TPU v7x, 32 devices: a whole 2x2x4 slice. The times are simulated.
32 devices in a mesh: tm: 8 (over y, x, core), shard: 4 (over z).
Axes of the slice: x: 2, y: 2, z: 4, core: 2. Of those that a mesh axis runs over, the one named last changes fastest.
Arguments:
- frames: bfloat16 [4096, 16384], P('tm', 'shard'), may hold values from -6 to 6
- gain: bfloat16 [256, 16384], P(None, 'shard'), may hold values from -0.0029296875 to 0.0029296875
- transition: float32 [256, 256], replicated, may hold values from -1 to 1
- smoother_gain: float32 [256, 256], replicated, may hold values from -1 to 1
- smoother_map: float32 [256, 256], replicated, may hold values from -9.1552734e-05 to 9.1552734e-05
- emission: bfloat16 [256, 16384], P(None, 'shard'), may hold values from -0.09375 to 0.09375
- noise_precision: float32 [16384], P('shard'), may hold values from 0.5 to 4
Outputs:
- smoothed: float32 [4096, 256], P('tm')
- gradient: float32 [256, 16384], P('tm', 'shard')
All inputs are finite; a program needn't handle non-finite values.
Results may differ from a plain program's by a relative error of at most 0.0014.
Values sent between devices are 32-bit elements; how exact they have to be, the bound alone decides.
A program may use at most 128 MiB of HBM per device.

v0:
```python
import functools

import jax
import jax.numpy as jnp
from jax import lax
from jax.experimental import pallas as pl
from jax.experimental.pallas import tpu as pltpu
from jax.sharding import PartitionSpec as P

MESH = pl.DeviceIdType.MESH
CHUNKS = 4


def bits_of(count):
    return count.bit_length() - 1


def split(value):
    high = value.astype(jnp.bfloat16)
    low = (value - high.astype(jnp.float32)).astype(jnp.bfloat16)
    return high, low


def dot(a, b):
    return jnp.dot(a, b, preferred_element_type=jnp.float32)


def dot3(value, right_high, right_low):
    high, low = split(value)
    return dot(high, right_high) + (dot(low, right_high) + dot(high, right_low))


def row_ids(count):
    return lax.broadcasted_iota(jnp.int32, (count, 1), 0)


def kernel(
    T, S,
    frames, gain, transition, smoother_gain, smoother_map, emission, noise,
    smoothed_out, gradient_out,
    part, landed, state, carry_buf, power, fh, fl, gh, gl, ends_f, ends_s, low, low_t, acc, *rest,
):
    stages = bits_of(T)
    inbox = rest[:stages]
    rs_send, rs_recv, ag_send, ag_recv, ef_send, ef_recv, es_send, es_recv, gr_send, gr_recv = rest[stages:]
    L, features = frames.shape
    lat = gain.shape[0]
    rows = L // S
    levels = bits_of(L)
    mt, ms = lax.axis_index("tm"), lax.axis_index("shard")

    barrier = pltpu.get_barrier_semaphore()

    def greet_s(k, c):
        pl.semaphore_signal(barrier, inc=1, device_id=(mt, lax.rem(ms + k, S)), device_id_type=MESH)
        return c

    def greet_t(k, c):
        pl.semaphore_signal(barrier, inc=1, device_id=(lax.rem(mt + k, T), ms), device_id_type=MESH)
        return c

    lax.fori_loop(1, S, greet_s, 0)
    lax.fori_loop(1, T, greet_t, 0)

    def scatter_copy(k):
        return pltpu.make_async_remote_copy(
            src_ref=part.at[k], dst_ref=landed.at[k], send_sem=rs_send.at[k], recv_sem=rs_recv.at[k],
            device_id=(mt, lax.rem(ms + k, S)), device_id_type=MESH)

    def partial_drive(k):
        owner = lax.rem(ms + k, S)
        block = frames[pl.ds(pl.multiple_of(owner * rows, rows), rows), :]
        part[k] = lax.dot_general(block, gain[...], (((1,), (1,)), ((), ())), preferred_element_type=jnp.float32)

    def drive_step(k, c):
        partial_drive(k)

        @pl.when(k == 1)
        def _():
            pl.semaphore_wait(barrier, S - 1 + T - 1)

        scatter_copy(k).start()
        return c

    lax.fori_loop(1, S, drive_step, 0)
    partial_drive(0)

    power[0] = transition[...].T
    power[1] = smoother_gain[...].T
    fh[0], fl[0] = split(power[0])
    gh[0], gl[0] = split(power[1])

    def square(k, c):
        for i, (h, l) in enumerate(((fh, fl), (gh, gl))):
            value = jnp.dot(power[i], power[i], precision=lax.Precision.HIGHEST, preferred_element_type=jnp.float32)
            power[i] = value
            h[k + 1], l[k + 1] = split(value)
        return c

    lax.fori_loop(0, levels + stages - 1, square, 0)

    total = part[0]
    for k in range(1, S):
        scatter_copy(k).wait_recv()
        total = total + landed[k]
    mine = pl.ds(pl.multiple_of(ms * rows, rows), rows)
    state[mine, :] = total

    def gather_copy(k):
        return pltpu.make_async_remote_copy(
            src_ref=state.at[mine], dst_ref=state.at[mine], send_sem=ag_send.at[k], recv_sem=ag_recv.at[k],
            device_id=(mt, lax.rem(ms + k, S)), device_id_type=MESH)

    def gather_wait(k):
        source = lax.rem(ms + S - k, S)
        there = state.at[pl.ds(pl.multiple_of(source * rows, rows), rows)]
        pltpu.make_async_remote_copy(
            src_ref=there, dst_ref=there, send_sem=ag_send.at[k], recv_sem=ag_recv.at[k],
            device_id=(mt, lax.rem(ms + k, S)), device_id_type=MESH).wait_recv()

    for k in range(1, S):
        gather_copy(k).start()
    map_h, map_l = split(smoother_map[...].T)
    for k in range(1, S):
        gather_wait(k)
    for k in range(1, S):
        gather_copy(k).wait_send()
        scatter_copy(k).wait_send()

    ids = row_ids(L)

    def local_scan(h, l, backward):
        for level in range(levels):
            d = 1 << level
            if d < 8:
                y = dot3(state[...], h[level], l[level])
                if backward:
                    moved = jnp.where(ids < L - d, pltpu.roll(y, L - d, 0), 0.0)
                else:
                    moved = jnp.where(ids >= d, pltpu.roll(y, d, 0), 0.0)
                state[...] = state[...] + moved
            elif backward:
                y = dot3(state[d:, :], h[level], l[level])
                state[: L - d, :] = state[: L - d, :] + y
            else:
                y = dot3(state[: L - d, :], h[level], l[level])
                state[d:, :] = state[d:, :] + y

    def exchange(ends, edge, send, recv):
        ends[mt] = jnp.broadcast_to(edge, (8, lat))

        def copy(k):
            return pltpu.make_async_remote_copy(
                src_ref=ends.at[mt], dst_ref=ends.at[mt], send_sem=send.at[k], recv_sem=recv.at[k],
                device_id=(lax.rem(mt + k, T), ms), device_id_type=MESH)

        def arrive(k):
            source = lax.rem(mt + T - k, T)
            pltpu.make_async_remote_copy(
                src_ref=ends.at[source], dst_ref=ends.at[source], send_sem=send.at[k], recv_sem=recv.at[k],
                device_id=(lax.rem(mt + k, T), ms), device_id_type=MESH).wait_recv()

        for k in range(1, T):
            copy(k).start()
        for k in range(1, T):
            arrive(k)
        for k in range(1, T):
            copy(k).wait_send()
        value = jnp.concatenate([ends[t, 0:1, :] for t in range(T)], axis=0)
        return value

    def arriving(value, h, l, backward):
        small = row_ids(T)
        for level in range(stages):
            d = 1 << level
            y = dot3(value, h[levels + level], l[levels + level])
            if backward:
                y = jnp.where(small < T - d, pltpu.roll(y, T - d, 0), 0.0)
            else:
                y = jnp.where(small >= d, pltpu.roll(y, d, 0), 0.0)
            value = value + y
        pick = mt + 1 if backward else mt - 1
        return jnp.sum(jnp.where(small == pick, value, 0.0), axis=0, keepdims=True)

    def add_carry(carry, h, l, backward):
        small = row_ids(8)
        exponent = 7 - small if backward else small
        value = dot3(jnp.broadcast_to(carry, (8, lat)), h[0], l[0])
        for level in range(3):
            moved = dot3(value, h[level], l[level])
            value = jnp.where((exponent >> level) & 1 == 1, moved, value)
        if backward:
            carry_buf[L - 8 :, :] = value
        else:
            carry_buf[:8, :] = value
        for level in range(3, levels):
            d = 1 << level
            if backward:
                carry_buf[L - 2 * d : L - d, :] = dot3(carry_buf[L - d :, :], h[level], l[level])
            else:
                carry_buf[d : 2 * d, :] = dot3(carry_buf[:d, :], h[level], l[level])
        state[...] = state[...] + carry_buf[...]

    local_scan(fh, fl, False)
    ends = exchange(ends_f, state[L - 1 :, :], ef_send, ef_recv)
    add_carry(arriving(ends, fh, fl, False), fh, fl, False)

    filtered = state[...]
    own = dot3(filtered, map_h, map_l)
    final_row = (ids == L - 1) & (mt == T - 1)
    state[...] = jnp.where(final_row, filtered, own)

    local_scan(gh, gl, True)
    starts = exchange(ends_s, state[:1, :], es_send, es_recv)
    add_carry(arriving(starts, gh, gl, True), gh, gl, True)

    smoothed = state[...]
    smoothed_out[...] = smoothed
    low[...] = smoothed.astype(jnp.bfloat16)
    low_t[...] = smoothed.T.astype(jnp.bfloat16)

    width = features // CHUNKS
    share = lat // T

    def order(c):
        places = list(range(stages))
        return places if c % 2 == 0 else places[:1] + places[:0:-1]

    def bit(place):
        return lax.rem(lax.div(mt, 1 << place), 2)

    def offset(c, stage):
        where = 0
        for earlier in range(stage):
            where = where + bit(order(c)[earlier]) * (T >> (earlier + 1))
        return where

    def halving_copy(c, stage):
        place = order(c)[stage]
        b = bit(place)
        half = T >> (stage + 1)
        partner = mt + (1 - 2 * b) * (1 << place)
        return pltpu.make_async_remote_copy(
            src_ref=acc.at[c, pl.ds(offset(c, stage) + (1 - b) * half, half)],
            dst_ref=inbox[stage].at[c],
            send_sem=gr_send.at[stage, c], recv_sem=gr_recv.at[stage, c],
            device_id=(partner, ms), device_id_type=MESH)

    def compute(c):
        columns = slice(c * width, (c + 1) * width)
        predicted = dot(low[...], emission[:, columns])
        weighted = (noise[:, columns] * (frames[:, columns].astype(jnp.float32) - predicted)).astype(jnp.bfloat16)
        product = dot(low_t[...], weighted)
        for owner in range(T):
            where = 0
            for stage, place in enumerate(order(c)):
                where += (owner >> place & 1) * (T >> (stage + 1))
            acc[c, where] = product[owner * share : (owner + 1) * share, :]

    def take(c, stage):
        halving_copy(c, stage).wait_recv()
        half = T >> (stage + 1)
        keep = pl.ds(offset(c, stage + 1), half)
        acc[c, keep] = acc[c, keep] + inbox[stage][c]

    for step in range(CHUNKS + stages):
        if step < CHUNKS:
            compute(step)
            halving_copy(step, 0).start()
        for stage in range(stages):
            c = step - 1 - stage
            if 0 <= c < CHUNKS:
                take(c, stage)
                if stage + 1 < stages:
                    halving_copy(c, stage + 1).start()
                else:
                    gradient_out[:, c * width : (c + 1) * width] = acc[c, offset(c, stages)] / (L * T)
    for c in range(CHUNKS):
        for stage in range(stages):
            halving_copy(c, stage).wait_send()


def on_device(frames, gain, transition, smoother_gain, smoother_map, emission, noise_precision):
    T, S = lax.axis_size("tm"), lax.axis_size("shard")
    L, features = frames.shape
    lat = gain.shape[0]
    rows = L // S
    stages = bits_of(T)
    levels = bits_of(L) + stages
    width = features // CHUNKS
    f32, b16 = jnp.float32, jnp.bfloat16
    dma = pltpu.SemaphoreType.DMA
    scratch = [
        pltpu.VMEM((S, rows, lat), f32),
        pltpu.VMEM((S, rows, lat), f32),
        pltpu.VMEM((L, lat), f32),
        pltpu.VMEM((L, lat), f32),
        pltpu.VMEM((2, lat, lat), f32),
        pltpu.VMEM((levels, lat, lat), b16),
        pltpu.VMEM((levels, lat, lat), b16),
        pltpu.VMEM((levels, lat, lat), b16),
        pltpu.VMEM((levels, lat, lat), b16),
        pltpu.VMEM((T, 8, lat), f32),
        pltpu.VMEM((T, 8, lat), f32),
        pltpu.VMEM((L, lat), b16),
        pltpu.VMEM((lat, L), b16),
        pltpu.VMEM((CHUNKS, T, lat // T, width), f32),
    ]
    scratch += [pltpu.VMEM((CHUNKS, T >> (s + 1), lat // T, width), f32) for s in range(stages)]
    scratch += [dma((S,))] * 4 + [dma((T,))] * 4 + [dma((stages, CHUNKS))] * 2
    vmem = pl.BlockSpec(memory_space=pltpu.VMEM)
    flops = 6 * L * features * lat
    return pl.pallas_call(
        functools.partial(kernel, T, S),
        out_shape=(
            jax.ShapeDtypeStruct((L, lat), f32),
            jax.ShapeDtypeStruct((lat // T, features), f32),
        ),
        in_specs=[vmem] * 7,
        out_specs=(vmem, vmem),
        scratch_shapes=scratch,
        compiler_params=pltpu.CompilerParams(
            collective_id=0, has_side_effects=True, vmem_limit_bytes=56 * 1024 * 1024
        ),
        cost_estimate=pl.CostEstimate(flops=flops, bytes_accessed=2 * L * features, transcendentals=0),
    )(frames, gain, transition, smoother_gain, smoother_map, emission, noise_precision[None, :])


def solution(mesh):
    in_specs = (P("tm", "shard"), P(None, "shard"), P(), P(), P(), P(None, "shard"), P("shard"))
    out_specs = (P("tm", None), P("tm", "shard"))
    return jax.shard_map(
        on_device, mesh=mesh, in_specs=in_specs, out_specs=out_specs, check_vma=False
    )
```

profile of v0, /device:TPU:24, one launch (start us, length us, event | category | flops | bytes accessed | tf_op | source)
XLA Modules:
  0.0 84.9 jit_solution(3899528710971480533)
XLA Ops:
  0.6 80.5 %shard_map.86 = (f32[512,256]{1,0:T(8,128)}, f32[32,4096]{1,0:T(8,128)}) custom-call(bf16[512,4096]{1,0:T(8,128)(2,1)} %frames.1, bf16[256,4096]{1,0:T(8,128)(2,1)} %gain.1, f32[256,256]{1,0:T(8,128)} %transition.1, f32[256,256]{1,0:T(8,128)} %smoother_gain.1, f32[256,256]{1,0:T(8,128)} %smoother_map.1, bf16[256,4096]{1,0:T(8,128)(2,1)} %emission.1, ...), custom_call_target="tpu_custom_call" | custom-call | flops 3221225472 | bytes 4194304 | tf_op jit(solution)/shard_map/pallas_call | solution.py:313
  81.1 1.9 %copy.11 = f32[512,256]{1,0:T(8,128)} copy(f32[512,256]{1,0:T(8,128)} %get-tuple-element.4) | data formatting | bytes 1048576
  83.0 1.9 %copy.12 = f32[32,4096]{1,0:T(8,128)} copy(f32[32,4096]{1,0:T(8,128)} %get-tuple-element.5) | data formatting | bytes 1048576
where the time goes:
time: 85.1 us; the launch traced here: 84.9 us
  Pallas kernels  80.5 us (95%)
  local copies, waits for them, and re-layouts  3.74 us (4%)
    pallas_call x1, Pallas kernels, on_device(): pl.pallas_call(functools.partial(kernel, T, S), out_shape=(jax.ShapeDtype...  80.5 us
    unnamed x2, local copies, waits for them, and re-layouts  3.74 us

commit v1 on v0

--- a/solution.py
+++ b/solution.py
@@ -8,7 +8,7 @@
 from jax.sharding import PartitionSpec as P
 
 MESH = pl.DeviceIdType.MESH
-CHUNKS = 4
+CHUNKS = 8
 
 
 def bits_of(count):
@@ -36,15 +36,15 @@
 
 def kernel(
     T, S,
-    frames, gain, transition, smoother_gain, smoother_map, emission, noise,
+    frames_in, gain_in, transition, smoother_gain, smoother_map, emission_in, noise,
     smoothed_out, gradient_out,
-    part, landed, state, carry_buf, power, fh, fl, gh, gl, ends_f, ends_s, low, low_t, acc, *rest,
+    frames, gain, emission, part, landed, state, carry_buf, power, fh, fl, gh, gl, ends_f, ends_s, low, low_t, acc, *rest,
 ):
     stages = bits_of(T)
     inbox = rest[:stages]
-    rs_send, rs_recv, ag_send, ag_recv, ef_send, ef_recv, es_send, es_recv, gr_send, gr_recv = rest[stages:]
-    L, features = frames.shape
-    lat = gain.shape[0]
+    rs_send, rs_recv, ag_send, ag_recv, ef_send, ef_recv, es_send, es_recv, gr_send, gr_recv, block_sem, whole_sem = rest[stages:]
+    L, features = frames_in.shape
+    lat = gain_in.shape[0]
     rows = L // S
     levels = bits_of(L)
     mt, ms = lax.axis_index("tm"), lax.axis_index("shard")
@@ -58,6 +58,17 @@
     def greet_t(k, c):
         pl.semaphore_signal(barrier, inc=1, device_id=(lax.rem(mt + k, T), ms), device_id_type=MESH)
         return c
+
+    def block_copy(k):
+        there = pl.ds(pl.multiple_of(lax.rem(ms + k, S) * rows, rows), rows)
+        return pltpu.make_async_copy(frames_in.at[there], frames.at[there], block_sem.at[k])
+
+    gain_copy = pltpu.make_async_copy(gain_in, gain, whole_sem.at[0])
+    emission_copy = pltpu.make_async_copy(emission_in, emission, whole_sem.at[1])
+    gain_copy.start()
+    for k in list(range(1, S)) + [0]:
+        block_copy(k).start()
+    emission_copy.start()
 
     lax.fori_loop(1, S, greet_s, 0)
     lax.fori_loop(1, T, greet_t, 0)
@@ -68,6 +79,7 @@
             device_id=(mt, lax.rem(ms + k, S)), device_id_type=MESH)
 
     def partial_drive(k):
+        block_copy(k).wait()
         owner = lax.rem(ms + k, S)
         block = frames[pl.ds(pl.multiple_of(owner * rows, rows), rows), :]
         part[k] = lax.dot_general(block, gain[...], (((1,), (1,)), ((), ())), preferred_element_type=jnp.float32)
@@ -82,6 +94,7 @@
         scatter_copy(k).start()
         return c
 
+    gain_copy.wait()
     lax.fori_loop(1, S, drive_step, 0)
     partial_drive(0)
 
@@ -97,7 +110,8 @@
             h[k + 1], l[k + 1] = split(value)
         return c
 
-    lax.fori_loop(0, levels + stages - 1, square, 0)
+    early = (levels + stages - 1) // 2
+    lax.fori_loop(0, early, square, 0)
 
     total = part[0]
     for k in range(1, S):
@@ -120,6 +134,7 @@
 
     for k in range(1, S):
         gather_copy(k).start()
+    lax.fori_loop(early, levels + stages - 1, square, 0)
     map_h, map_l = split(smoother_map[...].T)
     for k in range(1, S):
         gather_wait(k)
@@ -219,6 +234,7 @@
     low[...] = smoothed.astype(jnp.bfloat16)
     low_t[...] = smoothed.T.astype(jnp.bfloat16)
 
+    emission_copy.wait()
     width = features // CHUNKS
     share = lat // T
 
@@ -291,6 +307,9 @@
     f32, b16 = jnp.float32, jnp.bfloat16
     dma = pltpu.SemaphoreType.DMA
     scratch = [
+        pltpu.VMEM((L, features), b16),
+        pltpu.VMEM((lat, features), b16),
+        pltpu.VMEM((lat, features), b16),
         pltpu.VMEM((S, rows, lat), f32),
         pltpu.VMEM((S, rows, lat), f32),
         pltpu.VMEM((L, lat), f32),
@@ -307,8 +326,9 @@
         pltpu.VMEM((CHUNKS, T, lat // T, width), f32),
     ]
     scratch += [pltpu.VMEM((CHUNKS, T >> (s + 1), lat // T, width), f32) for s in range(stages)]
-    scratch += [dma((S,))] * 4 + [dma((T,))] * 4 + [dma((stages, CHUNKS))] * 2
+    scratch += [dma((S,))] * 4 + [dma((T,))] * 4 + [dma((stages, CHUNKS))] * 2 + [dma((S,)), dma((2,))]
     vmem = pl.BlockSpec(memory_space=pltpu.VMEM)
+    hbm = pl.BlockSpec(memory_space=pl.ANY)
     flops = 6 * L * features * lat
     return pl.pallas_call(
         functools.partial(kernel, T, S),
@@ -316,7 +336,7 @@
             jax.ShapeDtypeStruct((L, lat), f32),
             jax.ShapeDtypeStruct((lat // T, features), f32),
         ),
-        in_specs=[vmem] * 7,
+        in_specs=[hbm, hbm, vmem, vmem, vmem, hbm, vmem],
         out_specs=(vmem, vmem),
         scratch_shapes=scratch,
         compiler_params=pltpu.CompilerParams(

time: 85.1 us -> 87 us (1.022)
  Pallas kernels: 80.5 us -> 82.4 us
    pallas_call x1, Pallas kernels: 80.5 us -> 82.4 us  [on_device(): pl.pallas_call(functools.partial(kernel, T, S), out_shape=(jax.ShapeDtype...]
where the time goes in v1:
time: 87 us; the launch traced here: 86.8 us
  Pallas kernels  82.4 us (95%)
  local copies, waits for them, and re-layouts  3.74 us (4%)
    pallas_call x1, Pallas kernels, on_device(): pl.pallas_call(functools.partial(kernel, T, S), out_shape=(jax.ShapeDtype...  82.4 us
    unnamed x2, local copies, waits for them, and re-layouts  3.74 us

profile of v1, /device:TPU:24, one launch (start us, length us, event | category | flops | bytes accessed | tf_op | source)
XLA Modules:
  0.0 86.8 jit_solution(16701074993934776964)
XLA Ops:
  0.6 82.4 %shard_map.86 = (f32[512,256]{1,0:T(8,128)}, f32[32,4096]{1,0:T(8,128)}) custom-call(bf16[512,4096]{1,0:T(8,128)(2,1)} %frames_in.1, bf16[256,4096]{1,0:T(8,128)(2,1)} %gain_in.1, f32[256,256]{1,0:T(8,128)} %transition.1, f32[256,256]{1,0:T(8,128)} %smoother_gain.1, f32[256,256]{1,0:T(8,128)} %smoother_map.1, bf16[256,4096]{1,0:T(8,128)(2,1)} %emission_in.1, ...), custom_call_target="tpu_custom_call" | custom-call | flops 3221225472 | bytes 4194304 | tf_op jit(solution)/shard_map/pallas_call | solution.py:333
  83.1 1.9 %copy.11 = f32[512,256]{1,0:T(8,128)} copy(f32[512,256]{1,0:T(8,128)} %get-tuple-element.4) | data formatting | bytes 1048576
  84.9 1.9 %copy.12 = f32[32,4096]{1,0:T(8,128)} copy(f32[32,4096]{1,0:T(8,128)} %get-tuple-element.5) | data formatting | bytes 1048576

commit v2 on v1

--- a/solution.py
+++ b/solution.py
@@ -8,7 +8,7 @@
 from jax.sharding import PartitionSpec as P
 
 MESH = pl.DeviceIdType.MESH
-CHUNKS = 8
+CHUNKS = 4
 
 
 def bits_of(count):
@@ -290,7 +290,7 @@
                 if stage + 1 < stages:
                     halving_copy(c, stage + 1).start()
                 else:
-                    gradient_out[:, c * width : (c + 1) * width] = acc[c, offset(c, stages)] / (L * T)
+                    gradient_out[:, c * width : (c + 1) * width] = acc[c, offset(c, stages)]
     for c in range(CHUNKS):
         for stage in range(stages):
             halving_copy(c, stage).wait_send()
@@ -330,7 +330,7 @@
     vmem = pl.BlockSpec(memory_space=pltpu.VMEM)
     hbm = pl.BlockSpec(memory_space=pl.ANY)
     flops = 6 * L * features * lat
-    return pl.pallas_call(
+    smoothed, total = pl.pallas_call(
         functools.partial(kernel, T, S),
         out_shape=(
             jax.ShapeDtypeStruct((L, lat), f32),
@@ -344,6 +344,7 @@
         ),
         cost_estimate=pl.CostEstimate(flops=flops, bytes_accessed=2 * L * features, transcendentals=0),
     )(frames, gain, transition, smoother_gain, smoother_map, emission, noise_precision[None, :])
+    return smoothed, total / (L * T)
 
 
 def solution(mesh):

time: 87 us -> 83.7 us (0.962)
  Pallas kernels: 82.4 us -> 79 us
  other arithmetic: 0 us -> 1.87 us
  local copies, waits for them, and re-layouts: 3.74 us -> 1.87 us
    pallas_call x1, Pallas kernels: 82.4 us -> 79 us  [on_device(): pl.pallas_call(functools.partial(kernel, T, S), out_shape=(jax.ShapeDtype...]
    div x0 -> x1, other arithmetic: none -> 1.87 us  [on_device(): return (smoothed, total / (L * T))]
    unnamed x2 -> x1, local copies, waits for them, and re-layouts: 3.74 us -> 1.87 us
where the time goes in v2:
time: 83.7 us; the launch traced here: 83.4 us
  Pallas kernels  79 us (94%)
  other arithmetic  1.87 us (2%)
  local copies, waits for them, and re-layouts  1.87 us (2%)
    pallas_call x1, Pallas kernels, on_device(): pl.pallas_call(functools.partial(kernel, T, S), out_shape=(jax.ShapeDtype...  79 us
    div x1, other arithmetic, on_device(): return (smoothed, total / (L * T))  1.87 us
    unnamed x1, local copies, waits for them, and re-layouts  1.87 us

profile of v2, /device:TPU:24, one launch (start us, length us, event | category | flops | bytes accessed | tf_op | source)
XLA Modules:
  0.0 83.4 jit_solution(8835097321781226381)
XLA Ops:
  0.6 79.0 %shard_map.86 = (f32[512,256]{1,0:T(8,128)}, f32[32,4096]{1,0:T(8,128)}) custom-call(bf16[512,4096]{1,0:T(8,128)(2,1)} %frames_in.1, bf16[256,4096]{1,0:T(8,128)(2,1)} %gain_in.1, f32[256,256]{1,0:T(8,128)} %transition.1, f32[256,256]{1,0:T(8,128)} %smoother_gain.1, f32[256,256]{1,0:T(8,128)} %smoother_map.1, bf16[256,4096]{1,0:T(8,128)(2,1)} %emission_in.1, ...), custom_call_target="tpu_custom_call" | custom-call | flops 3221225472 | bytes 4194304 | tf_op jit(solution)/shard_map/pallas_call | solution.py:333
  79.6 1.9 %broadcast_multiply_fusion = f32[32,4096]{1,0:T(8,128)} fusion(f32[32,4096]{1,0:T(8,128)} %get-tuple-element.5), kind=kLoop, calls=%fused_computation | loop fusion | flops 131072 | bytes 1048576 | tf_op jit(solution)/shard_map/div | solution.py:347
  81.5 1.9 %copy.10 = f32[512,256]{1,0:T(8,128)} copy(f32[512,256]{1,0:T(8,128)} %get-tuple-element.8) | data formatting | bytes 1048576
